TPU v7x, 128 devices: a whole 4x4x4 slice. The times are simulated.
128 devices in a mesh: gx: 32 (over z, x, core), gy: 4 (over y).
Axes of the slice: x: 4, y: 4, z: 4, core: 2. Of those that a mesh axis runs over, the one named last changes fastest.
Arguments:
- populations: float32 [19, 1024, 2048], P(None, 'gx', 'gy'), may hold values from 0 to 0.7, as said below
- positions: float32 [3072, 3, 642], P(('gx', 'gy')), may hold values from -3 to 31, as said below
- stiffness: float32 [3072], P(('gx', 'gy')), may hold values from 0.002 to 0.02
- membrane_shape: float32 [3, 642], replicated, may hold values from -6 to 6
- neighbours: int32 [642, 6], replicated, may hold values from 0 to 641, as said below
- home_tile: int32 [3072], P(('gx', 'gy')), may hold values from 0 to 127, as said below
Outputs:
- populations_out: float32 [19, 1024, 2048], P(None, 'gx', 'gy')
- displacement: float32 [3072, 3, 642], P(('gx', 'gy'))
- force_density: float32 [3, 1024, 2048], P(None, 'gx', 'gy')
Inputs may be any that keep to these rules, and one draw needn't show every extreme that they name: `populations`: every entry is positive. `positions`: the first coordinate lies within [1, 31], the second within [1, 31]; the third is taken modulo 16. `neighbours`: row v never names v. `home_tile`: cells are owned in blocks of 24 in gx+gy order; the home tile of a cell owned at gx index a has gx index a - 1, a or a + 1 (cyclically) and any gy index, numbered gx index times the number of gy devices plus gy index; at most 4 cells of one device share a home tile, and in every device some home tile has exactly 4 of them.
All inputs are finite; a program needn't handle non-finite values.
Results may differ from a plain program's by a relative error of at most 0.0022.
Values sent between devices are 32-bit elements; how exact they have to be, the bound alone decides.
A program may use at most 64 MiB of HBM per device.

v0:
```python
import functools

import jax
import jax.numpy as jnp
from jax import lax
from jax.experimental import pallas as pl
from jax.experimental.pallas import tpu as pltpu
from jax.sharding import PartitionSpec as P

CZ = 16
CAP = 4
STEPS = 2
GROUPS = 12
SELF = 4
WIDE = 768
MAIN = 640
LANES = CAP * MAIN + 128
CHUNKS = [(0, 512), (512, 512), (1024, 512), (1536, 512), (2048, 512), (2560, 128)]

VELOCITY = [
    (0, 0, 0),
    (1, 0, 0),
    (-1, 0, 0),
    (0, 1, 0),
    (0, -1, 0),
    (0, 0, 1),
    (0, 0, -1),
    (1, 1, 0),
    (-1, -1, 0),
    (1, -1, 0),
    (-1, 1, 0),
    (1, 0, 1),
    (-1, 0, -1),
    (1, 0, -1),
    (-1, 0, 1),
    (0, 1, 1),
    (0, -1, -1),
    (0, 1, -1),
    (0, -1, 1),
]
WEIGHT = [1.0 / 3.0] + [1.0 / 18.0] * 6 + [1.0 / 36.0] * 12
RIGHT_MOVERS = [1, 7, 9, 11, 13]
LEFT_MOVERS = [2, 8, 10, 12, 14]
UPWARD_MOVERS = [3, 7, 10, 15, 17]
DOWNWARD_MOVERS = [4, 8, 9, 16, 18]
EDGE_MOVERS = [(7, 24, 384), (8, 0, 0), (9, 24, 0), (10, 0, 384)]
RELAX_RATE = 1.25
PUSH_SCALE = 0.05
TETHER_GAIN = 2.0
MESH = pl.DeviceIdType.MESH
F32 = jnp.float32
BF16 = jnp.bfloat16


def signed_sum(parts):
    total = None
    for sign, value in parts:
        if sign == 0:
            continue
        if total is None:
            total = value if sign > 0 else -value
        else:
            total = total + value if sign > 0 else total - value
    return total


def moments(f):
    density = f[0]
    for q in range(1, 19):
        density = density + f[q]
    momentum = [signed_sum([(VELOCITY[q][c], f[q]) for q in range(1, 19)]) for c in range(3)]
    return density, momentum


def hat(row, count, first):
    grid = lax.broadcasted_iota(jnp.int32, (count, row.shape[1]), 0).astype(F32) + first
    return jnp.maximum(0.0, 1.0 - jnp.abs(row - grid))


def hat_z(row):
    wrapped = row - CZ * jnp.floor(row * (1.0 / CZ))
    grid = lax.broadcasted_iota(jnp.int32, (CZ, row.shape[1]), 0).astype(F32)
    gap = jnp.abs(wrapped - grid)
    return jnp.maximum(0.0, 1.0 - jnp.minimum(gap, CZ - gap))


def kernel(
    nx,
    ny,
    source_ref,
    stiff_ref,
    slot_ref,
    pops_ref,
    places_ref,
    shape_ref,
    near_ref,
    pops_out,
    moved_out,
    density_out,
    sendbuf,
    cells,
    drift,
    returned,
    matrix32,
    matrix,
    diagonal,
    shapes,
    forces,
    flat,
    table,
    lifted,
    total,
    post,
    velocity,
    x_send,
    y_send,
    e_send,
    x_recv,
    y_recv,
    e_recv,
    cell_send_sem,
    cell_recv_sem,
    back_send_sem,
    back_recv_sem,
    halo_send_sem,
    halo_recv_sem,
):
    me_x = lax.axis_index("gx")
    me_y = lax.axis_index("gy")
    vertices = places_ref.shape[2]

    def away(dx, dy):
        return (lax.rem(me_x + dx + nx, nx), lax.rem(me_y + dy + ny, ny))

    barrier = pltpu.get_barrier_semaphore()
    for g in range(GROUPS):
        if g != SELF:
            pl.semaphore_signal(barrier, inc=1, device_id=away(g // 4 - 1, g % 4), device_id_type=MESH)

    for g in range(GROUPS):
        into = cells if g == SELF else sendbuf
        into[g, 8:16, :] = jnp.zeros((8, WIDE), F32)
        for r in range(CAP):
            s = g * CAP + r
            into[g, 3 * r : 3 * r + 3, MAIN:WIDE] = jnp.full((3, 128), stiff_ref[s], F32)
            into[g, 3 * r : 3 * r + 3, 0:vertices] = places_ref[source_ref[s]]
    pl.semaphore_wait(barrier, GROUPS - 1)

    def cell_copy(g):
        return pltpu.make_async_remote_copy(
            src_ref=sendbuf.at[g],
            dst_ref=cells.at[g],
            send_sem=cell_send_sem.at[g],
            recv_sem=cell_recv_sem.at[g],
            device_id=away(g // 4 - 1, g % 4),
            device_id_type=MESH,
        )

    def back_copy(g):
        return pltpu.make_async_remote_copy(
            src_ref=drift.at[g],
            dst_ref=returned.at[g],
            send_sem=back_send_sem.at[g],
            recv_sem=back_recv_sem.at[g],
            device_id=away(1 - g // 4, ny - g % 4),
            device_id_type=MESH,
        )

    for g in (5, 7, 6, 0, 8, 1, 3, 9, 11, 2, 10):
        cell_copy(g).start()

    def link_rows(b, _):
        first = pl.multiple_of(b * 8, 8)
        rows = lax.broadcasted_iota(jnp.int32, (8, WIDE), 0) + first
        count = jnp.zeros((8, WIDE), F32)
        for n in range(6):
            count = count + jnp.where(near_ref[n : n + 1, :] == rows, 1.0, 0.0)
        matrix32[pl.ds(first, 8), :] = count
        return 0

    lax.fori_loop(0, WIDE // 8, link_rows, 0)
    degree = jnp.zeros((1, WIDE), F32)
    for b in range(WIDE // 128):
        both = matrix32[128 * b : 128 * b + 128, :] + matrix32[:, 128 * b : 128 * b + 128].T
        matrix[128 * b : 128 * b + 128, :] = both.astype(BF16)
        degree = degree + jnp.sum(both, axis=0, keepdims=True)
    inside = lax.broadcasted_iota(jnp.int32, (1, WIDE), 1) < vertices
    diagonal[...] = jnp.where(inside, degree + TETHER_GAIN, 0.0)
    shapes[...] = jnp.zeros_like(shapes)
    for r in range(CAP):
        shapes[3 * r : 3 * r + 3, 0:vertices] = shape_ref[...]

    def batch_force(b):
        x = cells[pl.ds(4 * b, 4)].reshape(64, WIDE)
        keep = lax.broadcasted_iota(jnp.int32, (64, WIDE), 1) < vertices
        center = jnp.sum(jnp.where(keep, x, 0.0), axis=1, keepdims=True) * (1.0 / vertices)
        shape = jnp.concatenate([shapes[...]] * 4, axis=0)
        strain = jnp.where(keep, x - center - shape, 0.0)
        high = strain.astype(BF16)
        rest = strain - high.astype(F32)
        middle = rest.astype(BF16)
        low = (rest - middle.astype(F32)).astype(BF16)
        parts = jnp.dot(
            jnp.concatenate([high, middle, low], axis=0), matrix[...], preferred_element_type=F32
        )
        linked = parts[0:64] + parts[64:128] + parts[128:192]
        pulled = strain * diagonal[...] - linked
        forces[...] = (-x[:, vertices : vertices + 1] * pulled).reshape(4, 16, WIDE)

    def flatten(block, into, g, row):
        lane = lax.broadcasted_iota(jnp.int32, (1, 128), 1)
        for c in range(3):
            tail = jnp.zeros((1, 128), F32)
            for r in range(CAP):
                into[g, row + c : row + c + 1, MAIN * r : MAIN * r + MAIN] = block[
                    3 * r + c : 3 * r + c + 1, 0:MAIN
                ]
                end = block[3 * r + c : 3 * r + c + 1, MAIN:WIDE]
                if r:
                    end = pltpu.roll(end, 2 * r, 1)
                tail = jnp.where((lane >= 2 * r) & (lane < 2 * r + 2), end, tail)
            into[g, row + c : row + c + 1, MAIN * CAP : LANES] = tail

    def spread_group(b, k):
        g = 4 * b + k
        flatten(cells[g], flat, g, 0)
        flatten(forces[k], flat, g, 3)
        acc = None
        for start, width in CHUNKS:
            for t in range(start, start + width, 128):
                at = slice(t, t + 128)
                along_x = hat(flat[g, 0:1, at], 32, 0.0)
                along_z = hat_z(flat[g, 2:3, at])
                y = jnp.broadcast_to(flat[g, 1:2, at], (16, 128))
                for j in range(32):
                    along_y = jnp.maximum(0.0, 1.0 - jnp.abs(y - float(j)))
                    table[g, 16 * j : 16 * j + 16, at] = (along_y * along_z).astype(BF16)
                for c in range(3):
                    lifted[32 * c : 32 * c + 32, at] = (flat[g, 3 + c : 4 + c, at] * along_x).astype(BF16)
            at = slice(start, start + width)
            part = lax.dot_general(
                lifted[:, at], table[g, :, at], (((1,), (1,)), ((), ())), preferred_element_type=F32
            )
            acc = part if acc is None else acc + part
        total[...] += acc

    def sample_group(g, add):
        lane = lax.broadcasted_iota(jnp.int32, (1, 128), 1)
        for start, width in CHUNKS:
            at = slice(start, start + width)
            picked = jnp.dot(velocity[...], table[g, :, at], preferred_element_type=F32)
            along_x = hat(flat[g, 0:1, at], 32, 0.0)
            for c in range(3):
                flat[g, 3 + c : 4 + c, at] = jnp.sum(
                    picked[32 * c : 32 * c + 32] * along_x, axis=0, keepdims=True
                )
        for c in range(3):
            tail = flat[g, 3 + c : 4 + c, MAIN * CAP : LANES]
            for r in range(CAP):
                row = slice(3 * r + c, 3 * r + c + 1)
                step = flat[g, 3 + c : 4 + c, MAIN * r : MAIN * r + MAIN]
                end = tail if r == 0 else pltpu.roll(tail, 128 - 2 * r, 1)
                end = jnp.where(lane < 2, end, 0.0)
                if add:
                    drift[g, row, 0:MAIN] += step
                    drift[g, row, MAIN:WIDE] += end
                else:
                    drift[g, row, 0:MAIN] = step
                    drift[g, row, MAIN:WIDE] = end
                    cells[g, row, 0:MAIN] += step
                    cells[g, row, MAIN:WIDE] += end

    def collide(from_ref):
        def rows(i, _):
            at_x = pl.ds(pl.multiple_of(8 * i, 8), 8)
            for t in range(0, 512, 128):
                at = slice(t, t + 128)
                f = [from_ref[q, at_x, at] for q in range(19)]
                push = [
                    PUSH_SCALE * total[pl.ds(pl.multiple_of(32 * c + 8 * i, 8), 8), at]
                    for c in range(3)
                ]
                density, momentum = moments(f)
                inverse = 1.0 / density
                u = [(momentum[c] + 0.5 * push[c]) * inverse for c in range(3)]
                square = u[0] * u[0] + u[1] * u[1] + u[2] * u[2]
                dot = u[0] * push[0] + u[1] * push[1] + u[2] * push[2]
                rate = RELAX_RATE * density
                half = 1.0 - 0.5 * RELAX_RATE
                base = rate * (1.0 - 1.5 * square) - (3.0 * half) * dot
                for q in range(19):
                    value = base
                    if q:
                        a = signed_sum([(VELOCITY[q][c], u[c]) for c in range(3)])
                        p = signed_sum([(VELOCITY[q][c], push[c]) for c in range(3)])
                        value = base + rate * a * (3.0 + 4.5 * a) + (half * p) * (3.0 + 9.0 * a)
                    post[q, at_x, at] = (1.0 - RELAX_RATE) * f[q] + WEIGHT[q] * value
            return 0

        lax.fori_loop(0, 4, rows, 0)

    def halo_copies(step):
        ends = (
            [(x_send, x_recv, side, (1, 0) if side == 0 else (-1, 0)) for side in range(2)]
            + [(y_send, y_recv, side, (0, 1) if side == 0 else (0, -1)) for side in range(2)]
            + [
                (e_send, e_recv, n, VELOCITY[EDGE_MOVERS[n][0]][:2])
                for n in range(4)
            ]
        )
        return [
            pltpu.make_async_remote_copy(
                src_ref=out.at[step, n],
                dst_ref=into.at[step, n],
                send_sem=halo_send_sem.at[8 * step + k],
                recv_sem=halo_recv_sem.at[8 * step + k],
                device_id=away(dx, dy),
                device_id_type=MESH,
            )
            for k, (out, into, n, (dx, dy)) in enumerate(ends)
        ]

    def exchange(step):
        lane = lax.broadcasted_iota(jnp.int32, (32, 128), 1)
        for n, (q, row, column) in enumerate(EDGE_MOVERS):
            e_send[step, n] = post[q, row : row + 8, column : column + 128]
        for side, (movers, row) in enumerate(((RIGHT_MOVERS, 31), (LEFT_MOVERS, 0))):
            x_send[step, side] = jnp.zeros((8, 512), F32)
            for n, q in enumerate(movers):
                x_send[step, side, n : n + 1, :] = post[q, row : row + 1, :]
        for side, (movers, column, turn) in enumerate(
            ((UPWARD_MOVERS, 384, 16), (DOWNWARD_MOVERS, 0, 0))
        ):
            face = jnp.zeros((32, 128), F32)
            for n, q in enumerate(movers):
                value = post[q, :, column : column + 128]
                shift = (16 * n + turn) % 128
                if shift:
                    value = pltpu.roll(value, shift, 1)
                face = jnp.where((lane >= 16 * n) & (lane < 16 * n + 16), value, face)
            y_send[step, side] = face
        copies = halo_copies(step)
        for copy in copies:
            copy.start()
        for copy in copies:
            copy.wait()

    def shift_rows(value, dx, edge):
        row = lax.broadcasted_iota(jnp.int32, value.shape, 0)
        if dx > 0:
            return jnp.where(row == 0, edge, pltpu.roll(value, 1, 0))
        return jnp.where(row == 31, edge, pltpu.roll(value, 31, 0))

    def stream(step):
        lane = lax.broadcasted_iota(jnp.int32, (32, 128), 1)
        layer = lax.broadcasted_iota(jnp.int32, (32, 512), 1) % CZ
        for q in range(19):
            dx, dy, dz = VELOCITY[q]
            value = post[q]
            if dx:
                side = 0 if dx > 0 else 1
                n = (RIGHT_MOVERS, LEFT_MOVERS)[side].index(q)
                value = shift_rows(value, dx, x_recv[step, side, n : n + 1, :])
            if dy:
                side = 0 if dy > 0 else 1
                n = (UPWARD_MOVERS, DOWNWARD_MOVERS)[side].index(q)
                rim = y_recv[step, side]
                turn = (128 - 16 * n) % 128 if dy > 0 else 112 - 16 * n
                if turn:
                    rim = pltpu.roll(rim, turn, 1)
                if dx:
                    at = [m[0] for m in EDGE_MOVERS].index(q)
                    row = 7 if dx > 0 else 0
                    edge = pltpu.roll(e_recv[step, at], 16 if dy > 0 else 112, 1)
                    rim = shift_rows(rim, dx, edge[row : row + 1, :])
                if dy > 0:
                    value = pltpu.roll(value, CZ, 1)
                    value = jnp.concatenate(
                        [jnp.where(lane < CZ, rim, value[:, 0:128]), value[:, 128:512]], axis=1
                    )
                else:
                    value = pltpu.roll(value, 512 - CZ, 1)
                    value = jnp.concatenate(
                        [value[:, 0:384], jnp.where(lane >= 112, rim, value[:, 384:512])], axis=1
                    )
            if dz > 0:
                value = jnp.where(layer == 0, pltpu.roll(value, CZ - 1 + 512 - 2 * (CZ - 1), 1), pltpu.roll(value, 1, 1))
            if dz < 0:
                value = jnp.where(layer == CZ - 1, pltpu.roll(value, CZ - 1, 1), pltpu.roll(value, 511, 1))
            pops_out[q] = value

        def rows(i, _):
            at_x = pl.ds(pl.multiple_of(16 * i, 16), 16)
            for t in range(0, 512, 128):
                at = slice(t, t + 128)
                density, momentum = moments([pops_out[q, at_x, at] for q in range(19)])
                inverse = 1.0 / density
                for c in range(3):
                    rows_c = pl.ds(pl.multiple_of(32 * c + 16 * i, 16), 16)
                    push = PUSH_SCALE * total[rows_c, at]
                    velocity[rows_c, at] = ((momentum[c] + 0.5 * push) * inverse).astype(BF16)
            return 0

        lax.fori_loop(0, 2, rows, 0)

    for step in range(STEPS):
        total[...] = jnp.zeros_like(total)
        for b in (1, 0, 2):
            if step == 0:
                for g in range(4 * b, 4 * b + 4):
                    if g != SELF:
                        cell_copy(g).wait_recv()
            batch_force(b)

            def one_spread(k, _):
                spread_group(b, k)
                return 0

            lax.fori_loop(0, 4, one_spread, 0)
        collide(pops_ref if step == 0 else pops_out)
        exchange(step)
        stream(step)
        if step < STEPS - 1:

            def one_sample(g, _):
                sample_group(g, False)
                return 0

            lax.fori_loop(0, GROUPS, one_sample, 0)
        else:
            density_out[...] = total[...].reshape(density_out.shape)

            def last_sample(i, _):
                g = lax.rem(i + SELF + 1, GROUPS)
                sample_group(g, True)
                back_copy(g).start()
                return 0

            lax.fori_loop(0, GROUPS - 1, last_sample, 0)
            sample_group(SELF, True)
            returned[SELF] = drift[SELF]

    for g in range(GROUPS):
        if g != SELF:
            back_copy(g).wait_recv()
    for n in range(places_ref.shape[0]):
        block = returned[slot_ref[n] // CAP]
        rank = slot_ref[n] % CAP
        value = block[0:3, 0:vertices]
        for r in range(1, CAP):
            value = jnp.where(rank == r, block[3 * r : 3 * r + 3, 0:vertices], value)
        moved_out[n] = value
    for g in range(GROUPS):
        if g != SELF:
            cell_copy(g).wait_send()
            back_copy(g).wait_send()


def local(populations, positions, stiffness, membrane_shape, neighbours, home_tile):
    nx = lax.axis_size("gx")
    ny = lax.axis_size("gy")
    cells = positions.shape[0]
    offset = jnp.mod(home_tile // ny - lax.axis_index("gx") + 1, nx)
    turn = jnp.mod(home_tile % ny - lax.axis_index("gy"), ny)
    order = jnp.arange(cells, dtype=jnp.int32)
    earlier = (home_tile[:, None] == home_tile[None, :]) & (order[None, :] < order[:, None])
    rank = jnp.sum(earlier.astype(jnp.int32), axis=1)
    slot = (offset * 4 + turn) * CAP + rank
    hit = slot[None, :] == jnp.arange(GROUPS * CAP, dtype=jnp.int32)[:, None]
    source = jnp.sum(jnp.where(hit, order[None, :], 0), axis=1)
    slot_stiffness = jnp.sum(jnp.where(hit, stiffness[None, :], 0.0), axis=1)
    near = jnp.pad(neighbours.T, ((0, 2), (0, WIDE - neighbours.shape[0])), constant_values=-1)
    width_x, plane = populations.shape[1:]
    smem = pl.BlockSpec(memory_space=pltpu.SMEM)
    vmem = pl.BlockSpec(memory_space=pltpu.VMEM)
    return pl.pallas_call(
        functools.partial(kernel, nx, ny),
        out_shape=(
            jax.ShapeDtypeStruct(populations.shape, F32),
            jax.ShapeDtypeStruct(positions.shape, F32),
            jax.ShapeDtypeStruct((3, width_x, plane), F32),
        ),
        in_specs=[smem] * 3 + [vmem] * 4,
        out_specs=(vmem, vmem, vmem),
        scratch_shapes=[
            pltpu.VMEM((GROUPS, 16, WIDE), F32),
            pltpu.VMEM((GROUPS, 16, WIDE), F32),
            pltpu.VMEM((GROUPS, 16, WIDE), F32),
            pltpu.VMEM((GROUPS, 16, WIDE), F32),
            pltpu.VMEM((WIDE, WIDE), F32),
            pltpu.VMEM((WIDE, WIDE), BF16),
            pltpu.VMEM((1, WIDE), F32),
            pltpu.VMEM((16, WIDE), F32),
            pltpu.VMEM((4, 16, WIDE), F32),
            pltpu.VMEM((GROUPS, 8, LANES), F32),
            pltpu.VMEM((GROUPS, plane, LANES), BF16),
            pltpu.VMEM((3 * width_x, LANES), BF16),
            pltpu.VMEM((3 * width_x, plane), F32),
            pltpu.VMEM(populations.shape, F32),
            pltpu.VMEM((3 * width_x, plane), BF16),
            pltpu.VMEM((STEPS, 2, 8, plane), F32),
            pltpu.VMEM((STEPS, 2, width_x, 128), F32),
            pltpu.VMEM((STEPS, 4, 8, 128), F32),
            pltpu.VMEM((STEPS, 2, 8, plane), F32),
            pltpu.VMEM((STEPS, 2, width_x, 128), F32),
            pltpu.VMEM((STEPS, 4, 8, 128), F32),
            pltpu.SemaphoreType.DMA((GROUPS,)),
            pltpu.SemaphoreType.DMA((GROUPS,)),
            pltpu.SemaphoreType.DMA((GROUPS,)),
            pltpu.SemaphoreType.DMA((GROUPS,)),
            pltpu.SemaphoreType.DMA((8 * STEPS,)),
            pltpu.SemaphoreType.DMA((8 * STEPS,)),
        ],
        compiler_params=pltpu.CompilerParams(
            collective_id=0, has_side_effects=True, vmem_limit_bytes=58 * 2**20
        ),
    )(source, slot_stiffness, slot, populations, positions, membrane_shape, near)


def solution(mesh):
    placed = (
        P(None, "gx", "gy"),
        P(("gx", "gy"), None, None),
        P(("gx", "gy")),
        P(),
        P(),
        P(("gx", "gy")),
    )
    return jax.shard_map(
        local,
        mesh=mesh,
        in_specs=placed,
        out_specs=(P(None, "gx", "gy"), P(("gx", "gy"), None, None), P(None, "gx", "gy")),
        check_vma=False,
    )
```

profile of v0, /device:TPU:0, one launch (start us, length us, event | category | flops | bytes accessed | tf_op | source)
XLA Modules:
  0.0 101.7 jit_solution(1614320194371469686)
XLA Ops:
  0.6 0.9 convert_reduce_fusion
  1.5 0.7 multiply_add_fusion.slot_ref
  2.2 0.0 copy-start.1
  2.2 1.3 %select_reduce_fusion.stiff_ref = f32[48]{0:T(128)} fusion(f32[24]{0:T(128)} %param.8, s32[24]{0:T(128)S(1)} %multiply_add_fusion.slot_ref), kind=kLoop, calls=%fused_computation | loop fusion | flops 3408 | bytes 384 | tf_op jit(solution)/shard_map/reduce_sum | solution.py:471
  3.6 0.6 select_reduce_fusion.1.source_ref
  4.2 1.3 %pad.4.near_ref = s32[8,768]{1,0:T(8,128)} pad(s32[6,642]{1,0:T(8,128)} %bitcast.1, s32[]{:T(128)} %constant.51.clone.1), padding=0_2x0_126 | pad | bytes 39988 | tf_op jit(solution)/shard_map/jit(_pad)/pad | solution.py:472
  5.5 1.8 %copy.11.places_ref = f32[24,3,642]{2,1,0:T(4,128)} copy(f32[24,3,642]{2,0,1:T(8,128)} %param.7) | data formatting | bytes 369792 | tf_op args[1]
  7.3 0.0 copy-done.1
  7.3 89.5 %shard_map.85 = (f32[19,32,512]{2,1,0:T(8,128)}, f32[24,3,642]{2,1,0:T(4,128)}, f32[3,32,512]{2,1,0:T(8,128)}) custom-call(s32[48]{0:T(128)} %select_reduce_fusion.1.source_ref, f32[48]{0:T(128)} %select_reduce_fusion.stiff_ref, s32[24]{0:T(128)} %copy-done.1, f32[19,32,512]{2,1,0:T(8,128)} %pops_ref.1, f32[24,3,642]{2,1,0:T(4,128)} %copy.11.places_ref, ...), custom_call_target="tpu_custom_call" | custom-call | tf_op jit(solution)/shard_map/pallas_call | solution.py:476
  96.8 1.7 %copy.12 = f32[24,3,642]{2,0,1:T(8,128)} copy(f32[24,3,642]{2,1,0:T(4,128)} %get-tuple-element.7) | data formatting | bytes 369792 | tf_op jit(solution)/shard_map/pallas_call | solution.py:476
  98.5 0.0 copy-start
  98.5 2.5 %copy.15 = f32[19,32,512]{2,1,0:T(8,128)} copy(f32[19,32,512]{2,1,0:T(8,128)} %get-tuple-element.12) | data formatting | bytes 2490368
  101.0 0.0 copy-done
  101.0 0.7 copy.16
Async XLA Ops:
  2.2 5.0 %copy-start.1 = (s32[24]{0:T(128)}, s32[24]{0:T(128)S(1)}, u32[]{:S(2)}) copy-start(s32[24]{0:T(128)S(1)} %multiply_add_fusion.slot_ref) | copy-start | bytes 292
  98.5 2.5 %copy-start = (f32[3,32,512]{2,1,0:T(8,128)S(1)}, f32[3,32,512]{2,1,0:T(8,128)}, u32[]{:S(2)}) copy-start(f32[3,32,512]{2,1,0:T(8,128)} %get-tuple-element.14) | copy-start | bytes 589828
where the time goes:
time: 103 us; the launch traced here: 102 us
  Pallas kernels  89.5 us (87%)
  local copies, waits for them, and re-layouts  7.98 us (8%)
  other arithmetic  3.51 us (3%)
    pallas_call x1, Pallas kernels, local(): pl.pallas_call(functools.partial(kernel, nx, ny), out_shape=(jax.ShapeDty...  89.5 us
    unnamed x7, local copies, waits for them, and re-layouts  4.94 us

commit v1 on v0

--- a/solution.py
+++ b/solution.py
@@ -11,10 +11,12 @@
 CAP = 4
 STEPS = 2
 GROUPS = 12
-SELF = 4
+SELF = 0
+BATCH = 3
 WIDE = 768
 MAIN = 640
 LANES = CAP * MAIN + 128
+MESSAGE = 1024
 CHUNKS = [(0, 512), (512, 512), (1024, 512), (1536, 512), (2048, 512), (2560, 128)]
 
 VELOCITY = [
@@ -84,23 +86,41 @@
     return jnp.maximum(0.0, 1.0 - jnp.minimum(gap, CZ - gap))
 
 
+def cut(value):
+    high = value.astype(BF16)
+    rest = value - high.astype(F32)
+    middle = rest.astype(BF16)
+    return high, middle, (rest - middle.astype(F32)).astype(BF16)
+
+
+def chosen(choice, rows):
+    parts = [jnp.dot(choice, part, preferred_element_type=F32) for part in cut(rows)]
+    return (parts[0] + parts[1]) + parts[2]
+
+
 def kernel(
     nx,
     ny,
-    source_ref,
-    stiff_ref,
-    slot_ref,
     pops_ref,
     places_ref,
+    stiff_ref,
+    home_ref,
     shape_ref,
     near_ref,
     pops_out,
     moved_out,
     density_out,
     sendbuf,
+    received,
+    backbuf,
+    returned,
     cells,
     drift,
-    returned,
+    gathered,
+    tails,
+    cell_rows,
+    places_pad,
+    near,
     matrix32,
     matrix,
     diagonal,
@@ -110,6 +130,8 @@
     table,
     lifted,
     total,
+    turned,
+    pops,
     post,
     velocity,
     x_send,
@@ -124,10 +146,15 @@
     back_recv_sem,
     halo_send_sem,
     halo_recv_sem,
+    local_sem,
 ):
+    load = pltpu.make_async_copy(pops_ref, pops, local_sem.at[0])
+    load.start()
     me_x = lax.axis_index("gx")
     me_y = lax.axis_index("gy")
     vertices = places_ref.shape[2]
+    near[...] = jnp.full((8, WIDE), -1, jnp.int32)
+    near[0:6, 0:vertices] = near_ref[...]
 
     def away(dx, dy):
         return (lax.rem(me_x + dx + nx, nx), lax.rem(me_y + dy + ny, ny))
@@ -135,38 +162,80 @@
     barrier = pltpu.get_barrier_semaphore()
     for g in range(GROUPS):
         if g != SELF:
-            pl.semaphore_signal(barrier, inc=1, device_id=away(g // 4 - 1, g % 4), device_id_type=MESH)
+            pl.semaphore_signal(barrier, inc=1, device_id=away((g % 3 + 1) % 3 - 1, g // 3), device_id_type=MESH)
+
+    count = places_ref.shape[1]
+    cell_rows[...] = jnp.full((8, 128), -1.0, F32)
+    cell_rows[0:1, 0:count] = home_ref[...].astype(F32)
+    cell_rows[1:2, 0:count] = stiff_ref[...]
+    home = jnp.broadcast_to(cell_rows[0:1, :], (128, 128))
+    across = lax.broadcasted_iota(jnp.int32, (128, 128), 1)
+    down = lax.broadcasted_iota(jnp.int32, (128, 128), 0)
+    earlier = (home == home.T) & (down < across)
+    rank = jnp.sum(jnp.where(earlier, 1.0, 0.0), axis=0, keepdims=True)
+    home = cell_rows[0:1, :]
+    tile_x = jnp.floor((home + 0.5) * (1.0 / ny))
+    offset = tile_x - (me_x - 1).astype(F32)
+    offset = jnp.where(offset < 0, offset + nx, offset)
+    offset = jnp.where(offset >= nx, offset - nx, offset)
+    turn = home - ny * tile_x - me_y.astype(F32)
+    turn = jnp.where(turn < 0, turn + ny, turn)
+    lane = lax.broadcasted_iota(jnp.int32, (1, 128), 1)
+    side = jnp.where(offset < 1, offset + 2, offset - 1)
+    slot = jnp.where(lane < count, (turn * 3 + side) * CAP + rank, -1.0)
+    hit = jnp.where(slot == down.astype(F32), 1.0, 0.0)
+    put = hit[0 : GROUPS * CAP, 0:32].astype(BF16)
+    take = hit.T[0:32, 0 : GROUPS * CAP].astype(BF16)
+    stiff = jnp.sum(hit * cell_rows[1:2, :], axis=1, keepdims=True)[0 : GROUPS * CAP]
+    places_pad[...] = jnp.zeros_like(places_pad)
+    for c in range(3):
+        places_pad[c, 0:count, 0:vertices] = places_ref[c]
+        gathered[c] = chosen(put, places_pad[c])
+    lanes = lax.broadcasted_iota(jnp.int32, (GROUPS * CAP, 128), 1)
+    tails[...] = jnp.where(
+        lanes < 2,
+        gathered[0, :, MAIN:WIDE],
+        jnp.where(
+            lanes < 4,
+            pltpu.roll(gathered[1, :, MAIN:WIDE], 2, 1),
+            jnp.where(lanes < 6, pltpu.roll(gathered[2, :, MAIN:WIDE], 4, 1), stiff),
+        ),
+    )
+
+    def fold(into, at, rows):
+        into[at, 0:4, 0:MAIN] = rows(0, 0, MAIN)
+        into[at, 4:8, 0:MAIN] = rows(1, 0, MAIN)
+        into[at, 0:4, 640:896] = rows(2, 0, 256)
+        into[at, 4:8, 640:896] = rows(2, 256, 512)
+        into[at, 0:4, 896:1024] = rows(2, 512, MAIN)
 
     for g in range(GROUPS):
-        into = cells if g == SELF else sendbuf
-        into[g, 8:16, :] = jnp.zeros((8, WIDE), F32)
-        for r in range(CAP):
-            s = g * CAP + r
-            into[g, 3 * r : 3 * r + 3, MAIN:WIDE] = jnp.full((3, 128), stiff_ref[s], F32)
-            into[g, 3 * r : 3 * r + 3, 0:vertices] = places_ref[source_ref[s]]
+        into = received if g == SELF else sendbuf
+        fold(into, g, lambda c, first, last, g=g: gathered[c, 4 * g : 4 * g + 4, first:last])
+        into[g, 4:8, 896:1024] = tails[4 * g : 4 * g + 4, :]
     pl.semaphore_wait(barrier, GROUPS - 1)
 
     def cell_copy(g):
         return pltpu.make_async_remote_copy(
             src_ref=sendbuf.at[g],
-            dst_ref=cells.at[g],
+            dst_ref=received.at[g],
             send_sem=cell_send_sem.at[g],
             recv_sem=cell_recv_sem.at[g],
-            device_id=away(g // 4 - 1, g % 4),
+            device_id=away((g % 3 + 1) % 3 - 1, g // 3),
             device_id_type=MESH,
         )
 
     def back_copy(g):
         return pltpu.make_async_remote_copy(
-            src_ref=drift.at[g],
+            src_ref=backbuf.at[g],
             dst_ref=returned.at[g],
             send_sem=back_send_sem.at[g],
             recv_sem=back_recv_sem.at[g],
-            device_id=away(1 - g // 4, ny - g % 4),
+            device_id=away(1 - (g % 3 + 1) % 3, ny - g // 3),
             device_id_type=MESH,
         )
 
-    for g in (5, 7, 6, 0, 8, 1, 3, 9, 11, 2, 10):
+    for g in (1, 2, 3, 9, 4, 10, 5, 11, 6, 7, 8):
         cell_copy(g).start()
 
     def link_rows(b, _):
@@ -174,7 +243,7 @@
         rows = lax.broadcasted_iota(jnp.int32, (8, WIDE), 0) + first
         count = jnp.zeros((8, WIDE), F32)
         for n in range(6):
-            count = count + jnp.where(near_ref[n : n + 1, :] == rows, 1.0, 0.0)
+            count = count + jnp.where(near[n : n + 1, :] == rows, 1.0, 0.0)
         matrix32[pl.ds(first, 8), :] = count
         return 0
 
@@ -187,25 +256,41 @@
     inside = lax.broadcasted_iota(jnp.int32, (1, WIDE), 1) < vertices
     diagonal[...] = jnp.where(inside, degree + TETHER_GAIN, 0.0)
     shapes[...] = jnp.zeros_like(shapes)
-    for r in range(CAP):
-        shapes[3 * r : 3 * r + 3, 0:vertices] = shape_ref[...]
+    for c in range(3):
+        shapes[4 * c : 4 * c + 4, 0:vertices] = jnp.broadcast_to(shape_ref[c : c + 1, :], (4, vertices))
+
+    def unfold(from_ref, g, put_rows):
+        put_rows(0, 0, MAIN, from_ref[g, 0:4, 0:MAIN])
+        put_rows(1, 0, MAIN, from_ref[g, 4:8, 0:MAIN])
+        put_rows(2, 0, 256, from_ref[g, 0:4, 640:896])
+        put_rows(2, 256, 512, from_ref[g, 4:8, 640:896])
+        put_rows(2, 512, MAIN, from_ref[g, 0:4, 896:1024])
+
+    def arrive(g):
+        def put_rows(c, first, last, value):
+            cells[g, 4 * c : 4 * c + 4, first:last] = value
+
+        unfold(received, g, put_rows)
+        tail = received[g, 4:8, 896:1024]
+        stiff = jnp.broadcast_to(tail[:, 6:7], (4, 128))
+        lanes = lax.broadcasted_iota(jnp.int32, (4, 128), 1)
+        for c in range(3):
+            end = pltpu.roll(tail, 128 - 2 * c, 1) if c else tail
+            cells[g, 4 * c : 4 * c + 4, MAIN:WIDE] = jnp.where(lanes < 2, end, stiff)
+        cells[g, 12:16, :] = jnp.zeros((4, WIDE), F32)
 
     def batch_force(b):
-        x = cells[pl.ds(4 * b, 4)].reshape(64, WIDE)
-        keep = lax.broadcasted_iota(jnp.int32, (64, WIDE), 1) < vertices
+        x = cells[BATCH * b : BATCH * b + BATCH].reshape(16 * BATCH, WIDE)
+        keep = lax.broadcasted_iota(jnp.int32, (16 * BATCH, WIDE), 1) < vertices
         center = jnp.sum(jnp.where(keep, x, 0.0), axis=1, keepdims=True) * (1.0 / vertices)
-        shape = jnp.concatenate([shapes[...]] * 4, axis=0)
+        shape = jnp.concatenate([shapes[...]] * BATCH, axis=0)
         strain = jnp.where(keep, x - center - shape, 0.0)
-        high = strain.astype(BF16)
-        rest = strain - high.astype(F32)
-        middle = rest.astype(BF16)
-        low = (rest - middle.astype(F32)).astype(BF16)
         parts = jnp.dot(
-            jnp.concatenate([high, middle, low], axis=0), matrix[...], preferred_element_type=F32
+            jnp.concatenate(cut(strain), axis=0), matrix[...], preferred_element_type=F32
         )
-        linked = parts[0:64] + parts[64:128] + parts[128:192]
+        linked = parts[0:48] + parts[48:96] + parts[96:144]
         pulled = strain * diagonal[...] - linked
-        forces[...] = (-x[:, vertices : vertices + 1] * pulled).reshape(4, 16, WIDE)
+        forces[...] = (-x[:, vertices : vertices + 1] * pulled).reshape(BATCH, 16, WIDE)
 
     def flatten(block, into, g, row):
         lane = lax.broadcasted_iota(jnp.int32, (1, 128), 1)
@@ -213,36 +298,30 @@
             tail = jnp.zeros((1, 128), F32)
             for r in range(CAP):
                 into[g, row + c : row + c + 1, MAIN * r : MAIN * r + MAIN] = block[
-                    3 * r + c : 3 * r + c + 1, 0:MAIN
+                    4 * c + r : 4 * c + r + 1, 0:MAIN
                 ]
-                end = block[3 * r + c : 3 * r + c + 1, MAIN:WIDE]
+                end = block[4 * c + r : 4 * c + r + 1, MAIN:WIDE]
                 if r:
                     end = pltpu.roll(end, 2 * r, 1)
                 tail = jnp.where((lane >= 2 * r) & (lane < 2 * r + 2), end, tail)
             into[g, row + c : row + c + 1, MAIN * CAP : LANES] = tail
 
     def spread_group(b, k):
-        g = 4 * b + k
+        g = BATCH * b + k
         flatten(cells[g], flat, g, 0)
         flatten(forces[k], flat, g, 3)
-        acc = None
-        for start, width in CHUNKS:
-            for t in range(start, start + width, 128):
-                at = slice(t, t + 128)
-                along_x = hat(flat[g, 0:1, at], 32, 0.0)
-                along_z = hat_z(flat[g, 2:3, at])
-                y = jnp.broadcast_to(flat[g, 1:2, at], (16, 128))
-                for j in range(32):
-                    along_y = jnp.maximum(0.0, 1.0 - jnp.abs(y - float(j)))
-                    table[g, 16 * j : 16 * j + 16, at] = (along_y * along_z).astype(BF16)
-                for c in range(3):
-                    lifted[32 * c : 32 * c + 32, at] = (flat[g, 3 + c : 4 + c, at] * along_x).astype(BF16)
-            at = slice(start, start + width)
-            part = lax.dot_general(
-                lifted[:, at], table[g, :, at], (((1,), (1,)), ((), ())), preferred_element_type=F32
-            )
-            acc = part if acc is None else acc + part
-        total[...] += acc
+        for t in range(0, LANES, 128):
+            at = slice(t, t + 128)
+            along_x = hat(flat[g, 0:1, at], 32, 0.0)
+            along_y = hat(flat[g, 1:2, at], 32, 0.0)
+            along_z = hat_z(flat[g, 2:3, at])
+            for j in range(32):
+                table[g, 16 * j : 16 * j + 16, at] = (along_y[j : j + 1] * along_z).astype(BF16)
+            for c in range(3):
+                lifted[32 * c : 32 * c + 32, at] = (flat[g, 3 + c : 4 + c, at] * along_x).astype(BF16)
+        turned[...] += lax.dot_general(
+            table[g], lifted[...], (((1,), (1,)), ((), ())), preferred_element_type=F32
+        )
 
     def sample_group(g, add):
         lane = lax.broadcasted_iota(jnp.int32, (1, 128), 1)
@@ -257,7 +336,7 @@
         for c in range(3):
             tail = flat[g, 3 + c : 4 + c, MAIN * CAP : LANES]
             for r in range(CAP):
-                row = slice(3 * r + c, 3 * r + c + 1)
+                row = slice(4 * c + r, 4 * c + r + 1)
                 step = flat[g, 3 + c : 4 + c, MAIN * r : MAIN * r + MAIN]
                 end = tail if r == 0 else pltpu.roll(tail, 128 - 2 * r, 1)
                 end = jnp.where(lane < 2, end, 0.0)
@@ -269,6 +348,14 @@
                     drift[g, row, MAIN:WIDE] = end
                     cells[g, row, 0:MAIN] += step
                     cells[g, row, MAIN:WIDE] += end
+
+    def give_back(into, g):
+        fold(into, g, lambda c, first, last: drift[g, 4 * c : 4 * c + 4, first:last])
+        lanes = lax.broadcasted_iota(jnp.int32, (4, 128), 1)
+        ends = [drift[g, 4 * c : 4 * c + 4, MAIN:WIDE] for c in range(3)]
+        into[g, 4:8, 896:1024] = jnp.where(
+            lanes < 2, ends[0], jnp.where(lanes < 4, pltpu.roll(ends[1], 2, 1), pltpu.roll(ends[2], 4, 1))
+        )
 
     def collide(from_ref):
         def rows(i, _):
@@ -387,13 +474,13 @@
                 value = jnp.where(layer == 0, pltpu.roll(value, CZ - 1 + 512 - 2 * (CZ - 1), 1), pltpu.roll(value, 1, 1))
             if dz < 0:
                 value = jnp.where(layer == CZ - 1, pltpu.roll(value, CZ - 1, 1), pltpu.roll(value, 511, 1))
-            pops_out[q] = value
+            pops[q] = value
 
         def rows(i, _):
             at_x = pl.ds(pl.multiple_of(16 * i, 16), 16)
             for t in range(0, 512, 128):
                 at = slice(t, t + 128)
-                density, momentum = moments([pops_out[q, at_x, at] for q in range(19)])
+                density, momentum = moments([pops[q, at_x, at] for q in range(19)])
                 inverse = 1.0 / density
                 for c in range(3):
                     rows_c = pl.ds(pl.multiple_of(32 * c + 16 * i, 16), 16)
@@ -404,20 +491,24 @@
         lax.fori_loop(0, 2, rows, 0)
 
     for step in range(STEPS):
-        total[...] = jnp.zeros_like(total)
-        for b in (1, 0, 2):
+        turned[...] = jnp.zeros_like(turned)
+        for b in (0, 1, 3, 2):
             if step == 0:
-                for g in range(4 * b, 4 * b + 4):
+                for g in range(BATCH * b, BATCH * b + BATCH):
                     if g != SELF:
                         cell_copy(g).wait_recv()
+                    arrive(g)
             batch_force(b)
 
             def one_spread(k, _):
                 spread_group(b, k)
                 return 0
 
-            lax.fori_loop(0, 4, one_spread, 0)
-        collide(pops_ref if step == 0 else pops_out)
+            lax.fori_loop(0, BATCH, one_spread, 0)
+        total[...] = turned[...].T
+        if step == 0:
+            load.wait()
+        collide(pops)
         exchange(step)
         stream(step)
         if step < STEPS - 1:
@@ -428,74 +519,108 @@
 
             lax.fori_loop(0, GROUPS, one_sample, 0)
         else:
-            density_out[...] = total[...].reshape(density_out.shape)
+            store_pops = pltpu.make_async_copy(pops, pops_out, local_sem.at[1])
+            store_pops.start()
+            stores = [
+                pltpu.make_async_copy(total.at[32 * c : 32 * c + 32], density_out.at[c], local_sem.at[2 + c])
+                for c in range(3)
+            ]
+            for store in stores:
+                store.start()
 
             def last_sample(i, _):
-                g = lax.rem(i + SELF + 1, GROUPS)
+                g = GROUPS - 1 - i
                 sample_group(g, True)
+                give_back(backbuf, g)
                 back_copy(g).start()
                 return 0
 
             lax.fori_loop(0, GROUPS - 1, last_sample, 0)
             sample_group(SELF, True)
-            returned[SELF] = drift[SELF]
+            give_back(returned, SELF)
 
     for g in range(GROUPS):
         if g != SELF:
             back_copy(g).wait_recv()
-    for n in range(places_ref.shape[0]):
-        block = returned[slot_ref[n] // CAP]
-        rank = slot_ref[n] % CAP
-        value = block[0:3, 0:vertices]
-        for r in range(1, CAP):
-            value = jnp.where(rank == r, block[3 * r : 3 * r + 3, 0:vertices], value)
-        moved_out[n] = value
+    for g in range(GROUPS):
+
+        def put_rows(c, first, last, value):
+            gathered[c, 4 * g : 4 * g + 4, first:last] = value
+
+        unfold(returned, g, put_rows)
+        tails[4 * g : 4 * g + 4, :] = returned[g, 4:8, 896:1024]
+    for c in range(3):
+        tail = tails[...]
+        gathered[c, :, MAIN:WIDE] = pltpu.roll(tail, 128 - 2 * c, 1) if c else tail
+        moved_out[c] = chosen(take, gathered[c])[0:count, 0:vertices]
+    store_pops.wait()
+    for store in stores:
+        store.wait()
     for g in range(GROUPS):
         if g != SELF:
             cell_copy(g).wait_send()
             back_copy(g).wait_send()
 
 
+def hand_out(a, b, c, a_out, b_out, c_out, a_held, b_held, c_held, in_sems, out_sems):
+    pieces = [(a, a_held, a_out, slice(q, min(q + 4, 19))) for q in range(0, 19, 4)]
+    pieces += [(b, b_held, b_out, slice(0, 3)), (c, c_held, c_out, slice(0, 3))]
+    loads = [
+        pltpu.make_async_copy(source.at[at], held.at[at], in_sems.at[n])
+        for n, (source, held, _, at) in enumerate(pieces)
+    ]
+    stores = [
+        pltpu.make_async_copy(held.at[at], target.at[at], out_sems.at[n])
+        for n, (_, held, target, at) in enumerate(pieces)
+    ]
+    for load in loads:
+        load.start()
+    for load, store in zip(loads, stores, strict=True):
+        load.wait()
+        store.start()
+    for store in stores:
+        store.wait()
+
+
 def local(populations, positions, stiffness, membrane_shape, neighbours, home_tile):
     nx = lax.axis_size("gx")
     ny = lax.axis_size("gy")
-    cells = positions.shape[0]
-    offset = jnp.mod(home_tile // ny - lax.axis_index("gx") + 1, nx)
-    turn = jnp.mod(home_tile % ny - lax.axis_index("gy"), ny)
-    order = jnp.arange(cells, dtype=jnp.int32)
-    earlier = (home_tile[:, None] == home_tile[None, :]) & (order[None, :] < order[:, None])
-    rank = jnp.sum(earlier.astype(jnp.int32), axis=1)
-    slot = (offset * 4 + turn) * CAP + rank
-    hit = slot[None, :] == jnp.arange(GROUPS * CAP, dtype=jnp.int32)[:, None]
-    source = jnp.sum(jnp.where(hit, order[None, :], 0), axis=1)
-    slot_stiffness = jnp.sum(jnp.where(hit, stiffness[None, :], 0.0), axis=1)
-    near = jnp.pad(neighbours.T, ((0, 2), (0, WIDE - neighbours.shape[0])), constant_values=-1)
+    places = positions.transpose(1, 0, 2)
     width_x, plane = populations.shape[1:]
-    smem = pl.BlockSpec(memory_space=pltpu.SMEM)
     vmem = pl.BlockSpec(memory_space=pltpu.VMEM)
-    return pl.pallas_call(
+    hbm = pl.BlockSpec(memory_space=pl.ANY)
+    populations, moved, density = pl.pallas_call(
         functools.partial(kernel, nx, ny),
         out_shape=(
             jax.ShapeDtypeStruct(populations.shape, F32),
-            jax.ShapeDtypeStruct(positions.shape, F32),
+            jax.ShapeDtypeStruct(places.shape, F32),
             jax.ShapeDtypeStruct((3, width_x, plane), F32),
         ),
-        in_specs=[smem] * 3 + [vmem] * 4,
-        out_specs=(vmem, vmem, vmem),
+        in_specs=[hbm] + [vmem] * 5,
+        out_specs=(hbm, vmem, hbm),
         scratch_shapes=[
+            pltpu.VMEM((GROUPS, 8, MESSAGE), F32),
+            pltpu.VMEM((GROUPS, 8, MESSAGE), F32),
+            pltpu.VMEM((GROUPS, 8, MESSAGE), F32),
+            pltpu.VMEM((GROUPS, 8, MESSAGE), F32),
             pltpu.VMEM((GROUPS, 16, WIDE), F32),
             pltpu.VMEM((GROUPS, 16, WIDE), F32),
-            pltpu.VMEM((GROUPS, 16, WIDE), F32),
-            pltpu.VMEM((GROUPS, 16, WIDE), F32),
+            pltpu.VMEM((3, GROUPS * CAP, WIDE), F32),
+            pltpu.VMEM((GROUPS * CAP, 128), F32),
+            pltpu.VMEM((8, 128), F32),
+            pltpu.VMEM((3, 32, WIDE), F32),
+            pltpu.VMEM((8, WIDE), jnp.int32),
             pltpu.VMEM((WIDE, WIDE), F32),
             pltpu.VMEM((WIDE, WIDE), BF16),
             pltpu.VMEM((1, WIDE), F32),
             pltpu.VMEM((16, WIDE), F32),
-            pltpu.VMEM((4, 16, WIDE), F32),
+            pltpu.VMEM((BATCH, 16, WIDE), F32),
             pltpu.VMEM((GROUPS, 8, LANES), F32),
             pltpu.VMEM((GROUPS, plane, LANES), BF16),
             pltpu.VMEM((3 * width_x, LANES), BF16),
             pltpu.VMEM((3 * width_x, plane), F32),
+            pltpu.VMEM((plane, 3 * width_x), F32),
+            pltpu.VMEM(populations.shape, F32),
             pltpu.VMEM(populations.shape, F32),
             pltpu.VMEM((3 * width_x, plane), BF16),
             pltpu.VMEM((STEPS, 2, 8, plane), F32),
@@ -510,11 +635,22 @@
             pltpu.SemaphoreType.DMA((GROUPS,)),
             pltpu.SemaphoreType.DMA((8 * STEPS,)),
             pltpu.SemaphoreType.DMA((8 * STEPS,)),
+            pltpu.SemaphoreType.DMA((5,)),
         ],
         compiler_params=pltpu.CompilerParams(
             collective_id=0, has_side_effects=True, vmem_limit_bytes=58 * 2**20
         ),
-    )(source, slot_stiffness, slot, populations, positions, membrane_shape, near)
+    )(populations, places, stiffness[None], home_tile[None], membrane_shape, neighbours.T)
+    results = (populations, moved, density)
+    populations, moved, density = pl.pallas_call(
+        hand_out,
+        out_shape=tuple(jax.ShapeDtypeStruct(r.shape, F32) for r in results),
+        in_specs=[hbm] * 3,
+        out_specs=(hbm,) * 3,
+        scratch_shapes=[pltpu.VMEM(r.shape, F32) for r in results]
+        + [pltpu.SemaphoreType.DMA((7,)), pltpu.SemaphoreType.DMA((7,))],
+    )(*results)
+    return populations, moved.transpose(1, 0, 2), density
 
 
 def solution(mesh):

time: 103 us -> 82.4 us (0.80); the launches traced: 102 us -> 82.3 us
  Pallas kernels: 89.5 us -> 81.5 us
  local copies, waits for them, and re-layouts: 7.98 us -> 0 us
  other arithmetic: 3.51 us -> 0 us
    pallas_call x1, Pallas kernels: 89.5 us -> 79.3 us  [local(): pl.pallas_call(functools.partial(kernel, nx, ny), out_shape=(jax.ShapeDty...]
    unnamed x7 -> x0, local copies, waits for them, and re-layouts: 4.94 us -> none
    reduce_sum x3 -> x0, other arithmetic: 2.83 us -> none  [the longest x1 1.32 us: local(): slot_stiffness = jnp.sum(jnp.where(hit, stiffness[None, :], 0.0), axis=1)]
    pallas_call x0 -> x1, Pallas kernels: none -> 2.23 us  [local(): pl.pallas_call(hand_out, out_shape=tuple((jax.ShapeDtypeStruct(r.shape, F...]
    pallas_call x1 -> x0, local copies, waits for them, and re-layouts: 1.69 us -> none  [local(): pl.pallas_call(functools.partial(kernel, nx, ny), out_shape=(jax.ShapeDty...]
    pad x1 -> x0, local copies, waits for them, and re-layouts: 1.35 us -> none  [local(): jnp.pad(neighbours.T, ((0, 2), (0, WIDE - neighbours.shape[0])), constant...]
where the time goes in v1:
time: 82.4 us; the launch traced here: 82.3 us
  Pallas kernels  81.5 us (99%)
    pallas_call x1, Pallas kernels, local(): pl.pallas_call(functools.partial(kernel, nx, ny), out_shape=(jax.ShapeDty...  79.3 us
    pallas_call x1, Pallas kernels, local(): pl.pallas_call(hand_out, out_shape=tuple((jax.ShapeDtypeStruct(r.shape, F...  2.23 us

profile of v1, /device:TPU:0, one launch (start us, length us, event | category | flops | bytes accessed | tf_op | source)
XLA Modules:
  0.0 82.3 jit_solution(17891806573677948316)
XLA Ops:
  0.6 79.3 %shard_map.85 = (f32[19,32,512]{2,1,0:T(8,128)}, f32[3,24,642]{2,1,0:T(8,128)}, f32[3,32,512]{2,1,0:T(8,128)}) custom-call(f32[19,32,512]{2,1,0:T(8,128)} %pops_ref.1, f32[3,24,642]{2,1,0:T(8,128)} %bitcast.5, f32[1,24]{1,0:T(1,128)} %bitcast.7, s32[1,24]{1,0:T(1,128)} %bitcast.8, f32[3,642]{1,0:T(4,128)} %shape_ref.1, s32[6,642]{1,0:T(8,128)} %bitcast.6), custom_call_target="tpu_custom_call" | custom-call | tf_op jit(solution)/shard_map/pallas_call | solution.py:592
  79.9 2.2 %shard_map.86 = (f32[19,32,512]{2,1,0:T(8,128)}, f32[3,24,642]{2,1,0:T(8,128)}, f32[3,32,512]{2,1,0:T(8,128)}) custom-call(f32[19,32,512]{2,1,0:T(8,128)} %get-tuple-element.9.a, f32[3,24,642]{2,1,0:T(8,128)} %get-tuple-element.10.b, f32[3,32,512]{2,1,0:T(8,128)} %get-tuple-element.11.c), custom_call_target="tpu_custom_call" | custom-call | tf_op jit(solution)/shard_map/pallas_call | solution.py:645

commit v2 on v1

--- a/solution.py
+++ b/solution.py
@@ -12,12 +12,12 @@
 STEPS = 2
 GROUPS = 12
 SELF = 0
-BATCH = 3
+BATCHES = [(0, 1), (1, 2), (3, 3), (9, 3), (6, 3)]
 WIDE = 768
 MAIN = 640
-LANES = CAP * MAIN + 128
+LANES = CAP * MAIN
 MESSAGE = 1024
-CHUNKS = [(0, 512), (512, 512), (1024, 512), (1536, 512), (2048, 512), (2560, 128)]
+CHUNKS = [(start, 512) for start in range(0, LANES, 512)]
 
 VELOCITY = [
     (0, 0, 0),
@@ -127,7 +127,9 @@
     shapes,
     forces,
     flat,
+    flat_tail,
     table,
+    table_tail,
     lifted,
     total,
     turned,
@@ -256,6 +258,7 @@
     inside = lax.broadcasted_iota(jnp.int32, (1, WIDE), 1) < vertices
     diagonal[...] = jnp.where(inside, degree + TETHER_GAIN, 0.0)
     shapes[...] = jnp.zeros_like(shapes)
+    flat_tail[...] = jnp.zeros_like(flat_tail)
     for c in range(3):
         shapes[4 * c : 4 * c + 4, 0:vertices] = jnp.broadcast_to(shape_ref[c : c + 1, :], (4, vertices))
 
@@ -279,62 +282,92 @@
             cells[g, 4 * c : 4 * c + 4, MAIN:WIDE] = jnp.where(lanes < 2, end, stiff)
         cells[g, 12:16, :] = jnp.zeros((4, WIDE), F32)
 
-    def batch_force(b):
-        x = cells[BATCH * b : BATCH * b + BATCH].reshape(16 * BATCH, WIDE)
-        keep = lax.broadcasted_iota(jnp.int32, (16 * BATCH, WIDE), 1) < vertices
+    def batch_force(first, many):
+        rows = 16 * many
+        x = cells[first : first + many].reshape(rows, WIDE)
+        keep = lax.broadcasted_iota(jnp.int32, (rows, WIDE), 1) < vertices
         center = jnp.sum(jnp.where(keep, x, 0.0), axis=1, keepdims=True) * (1.0 / vertices)
-        shape = jnp.concatenate([shapes[...]] * BATCH, axis=0)
+        shape = jnp.concatenate([shapes[...]] * many, axis=0)
         strain = jnp.where(keep, x - center - shape, 0.0)
         parts = jnp.dot(
             jnp.concatenate(cut(strain), axis=0), matrix[...], preferred_element_type=F32
         )
-        linked = parts[0:48] + parts[48:96] + parts[96:144]
+        linked = parts[0:rows] + parts[rows : 2 * rows] + parts[2 * rows : 3 * rows]
         pulled = strain * diagonal[...] - linked
-        forces[...] = (-x[:, vertices : vertices + 1] * pulled).reshape(BATCH, 16, WIDE)
-
-    def flatten(block, into, g, row):
+        forces[first : first + many] = (-x[:, vertices : vertices + 1] * pulled).reshape(many, 16, WIDE)
+
+    def flatten(block, g, row):
         lane = lax.broadcasted_iota(jnp.int32, (1, 128), 1)
         for c in range(3):
             tail = jnp.zeros((1, 128), F32)
             for r in range(CAP):
-                into[g, row + c : row + c + 1, MAIN * r : MAIN * r + MAIN] = block[
+                flat[g, row + c : row + c + 1, MAIN * r : MAIN * r + MAIN] = block[
                     4 * c + r : 4 * c + r + 1, 0:MAIN
                 ]
                 end = block[4 * c + r : 4 * c + r + 1, MAIN:WIDE]
                 if r:
                     end = pltpu.roll(end, 2 * r, 1)
                 tail = jnp.where((lane >= 2 * r) & (lane < 2 * r + 2), end, tail)
-            into[g, row + c : row + c + 1, MAIN * CAP : LANES] = tail
-
-    def spread_group(b, k):
-        g = BATCH * b + k
-        flatten(cells[g], flat, g, 0)
-        flatten(forces[k], flat, g, 3)
+            tail = pltpu.roll(tail, 8 * g, 1)
+            mine = (lane >= 8 * g) & (lane < 8 * g + 8)
+            flat_tail[row + c : row + c + 1, :] = jnp.where(mine, tail, flat_tail[row + c : row + c + 1, :])
+
+    def tabulate(read, put_table, put_lifted, at):
+        along_x = hat(read(0, at), 32, 0.0)
+        along_y = hat(read(1, at), 32, 0.0)
+        along_z = hat_z(read(2, at))
+        for j in range(32):
+            put_table(j, at, (along_y[j : j + 1] * along_z).astype(BF16))
+        for c in range(3):
+            put_lifted(c, at, (read(3 + c, at) * along_x).astype(BF16))
+
+    def put_lifted(c, at, value):
+        lifted[32 * c : 32 * c + 32, at] = value
+
+    def spread_group(g):
+        flatten(cells[g], g, 0)
+        flatten(forces[g], g, 3)
+
+        def put_table(j, at, value):
+            table[g, 16 * j : 16 * j + 16, at] = value
+
         for t in range(0, LANES, 128):
-            at = slice(t, t + 128)
-            along_x = hat(flat[g, 0:1, at], 32, 0.0)
-            along_y = hat(flat[g, 1:2, at], 32, 0.0)
-            along_z = hat_z(flat[g, 2:3, at])
-            for j in range(32):
-                table[g, 16 * j : 16 * j + 16, at] = (along_y[j : j + 1] * along_z).astype(BF16)
-            for c in range(3):
-                lifted[32 * c : 32 * c + 32, at] = (flat[g, 3 + c : 4 + c, at] * along_x).astype(BF16)
+            tabulate(lambda n, at: flat[g, n : n + 1, at], put_table, put_lifted, slice(t, t + 128))
         turned[...] += lax.dot_general(
             table[g], lifted[...], (((1,), (1,)), ((), ())), preferred_element_type=F32
         )
+
+    def spread_tail():
+        def put_table(j, at, value):
+            table_tail[16 * j : 16 * j + 16, at] = value
+
+        at = slice(0, 128)
+        tabulate(lambda n, at: flat_tail[n : n + 1, at], put_table, put_lifted, at)
+        turned[...] += lax.dot_general(
+            table_tail[...], lifted[:, at], (((1,), (1,)), ((), ())), preferred_element_type=F32
+        )
+
+    def drifts(picked, row):
+        along_x = hat(row, 32, 0.0)
+        return [
+            jnp.sum(picked[32 * c : 32 * c + 32] * along_x, axis=0, keepdims=True) for c in range(3)
+        ]
+
+    def sample_tail():
+        picked = jnp.dot(velocity[...], table_tail[...], preferred_element_type=F32)
+        used = lax.broadcasted_iota(jnp.int32, (1, 128), 1) < 8 * GROUPS
+        for c, value in enumerate(drifts(picked, flat_tail[0:1, :])):
+            flat_tail[3 + c : 4 + c, :] = jnp.where(used, value, 0.0)
 
     def sample_group(g, add):
         lane = lax.broadcasted_iota(jnp.int32, (1, 128), 1)
         for start, width in CHUNKS:
             at = slice(start, start + width)
             picked = jnp.dot(velocity[...], table[g, :, at], preferred_element_type=F32)
-            along_x = hat(flat[g, 0:1, at], 32, 0.0)
-            for c in range(3):
-                flat[g, 3 + c : 4 + c, at] = jnp.sum(
-                    picked[32 * c : 32 * c + 32] * along_x, axis=0, keepdims=True
-                )
+            for c, value in enumerate(drifts(picked, flat[g, 0:1, at])):
+                flat[g, 3 + c : 4 + c, at] = value
         for c in range(3):
-            tail = flat[g, 3 + c : 4 + c, MAIN * CAP : LANES]
+            tail = pltpu.roll(flat_tail[3 + c : 4 + c, :], 128 - 8 * g, 1)
             for r in range(CAP):
                 row = slice(4 * c + r, 4 * c + r + 1)
                 step = flat[g, 3 + c : 4 + c, MAIN * r : MAIN * r + MAIN]
@@ -429,8 +462,7 @@
         copies = halo_copies(step)
         for copy in copies:
             copy.start()
-        for copy in copies:
-            copy.wait()
+        return copies
 
     def shift_rows(value, dx, edge):
         row = lax.broadcasted_iota(jnp.int32, value.shape, 0)
@@ -438,16 +470,37 @@
             return jnp.where(row == 0, edge, pltpu.roll(value, 1, 0))
         return jnp.where(row == 31, edge, pltpu.roll(value, 31, 0))
 
-    def stream(step):
-        lane = lax.broadcasted_iota(jnp.int32, (32, 128), 1)
-        layer = lax.broadcasted_iota(jnp.int32, (32, 512), 1) % CZ
+    def shift_layers(value, dz):
+        if dz == 0:
+            return value
+        width = value.shape[1]
+        layer = lax.broadcasted_iota(jnp.int32, value.shape, 1) % CZ
+        rim, wrap = (0, width + 1 - CZ) if dz > 0 else (CZ - 1, CZ - 1)
+        near_by = pltpu.roll(value, 1 if dz > 0 else width - 1, 1)
+        return jnp.where(layer == rim, pltpu.roll(value, wrap, 1), near_by)
+
+    def stream(step, copies):
         for q in range(19):
             dx, dy, dz = VELOCITY[q]
             value = post[q]
             if dx:
+                value = pltpu.roll(value, 1 if dx > 0 else 31, 0)
+            if dy:
+                value = pltpu.roll(value, CZ if dy > 0 else 512 - CZ, 1)
+            pops[q] = shift_layers(value, dz)
+        for copy in copies:
+            copy.wait()
+        lane = lax.broadcasted_iota(jnp.int32, (32, 128), 1)
+        for q in range(19):
+            dx, dy, dz = VELOCITY[q]
+            if dx:
                 side = 0 if dx > 0 else 1
                 n = (RIGHT_MOVERS, LEFT_MOVERS)[side].index(q)
-                value = shift_rows(value, dx, x_recv[step, side, n : n + 1, :])
+                row = 0 if dx > 0 else 31
+                edge = x_recv[step, side, n : n + 1, :]
+                if dy:
+                    edge = pltpu.roll(edge, CZ if dy > 0 else 512 - CZ, 1)
+                pops[q, row : row + 1, :] = shift_layers(edge, dz)
             if dy:
                 side = 0 if dy > 0 else 1
                 n = (UPWARD_MOVERS, DOWNWARD_MOVERS)[side].index(q)
@@ -460,21 +513,11 @@
                     row = 7 if dx > 0 else 0
                     edge = pltpu.roll(e_recv[step, at], 16 if dy > 0 else 112, 1)
                     rim = shift_rows(rim, dx, edge[row : row + 1, :])
+                rim = shift_layers(rim, dz)
                 if dy > 0:
-                    value = pltpu.roll(value, CZ, 1)
-                    value = jnp.concatenate(
-                        [jnp.where(lane < CZ, rim, value[:, 0:128]), value[:, 128:512]], axis=1
-                    )
+                    pops[q, :, 0:128] = jnp.where(lane < CZ, rim, pops[q, :, 0:128])
                 else:
-                    value = pltpu.roll(value, 512 - CZ, 1)
-                    value = jnp.concatenate(
-                        [value[:, 0:384], jnp.where(lane >= 112, rim, value[:, 384:512])], axis=1
-                    )
-            if dz > 0:
-                value = jnp.where(layer == 0, pltpu.roll(value, CZ - 1 + 512 - 2 * (CZ - 1), 1), pltpu.roll(value, 1, 1))
-            if dz < 0:
-                value = jnp.where(layer == CZ - 1, pltpu.roll(value, CZ - 1, 1), pltpu.roll(value, 511, 1))
-            pops[q] = value
+                    pops[q, :, 384:512] = jnp.where(lane >= 128 - CZ, rim, pops[q, :, 384:512])
 
         def rows(i, _):
             at_x = pl.ds(pl.multiple_of(16 * i, 16), 16)
@@ -492,25 +535,27 @@
 
     for step in range(STEPS):
         turned[...] = jnp.zeros_like(turned)
-        for b in (0, 1, 3, 2):
+        for first, many in BATCHES if step == 0 else [(0, GROUPS)]:
             if step == 0:
-                for g in range(BATCH * b, BATCH * b + BATCH):
+                for g in range(first, first + many):
                     if g != SELF:
                         cell_copy(g).wait_recv()
                     arrive(g)
-            batch_force(b)
-
-            def one_spread(k, _):
-                spread_group(b, k)
+            batch_force(first, many)
+
+            def one_spread(g, _):
+                spread_group(g)
                 return 0
 
-            lax.fori_loop(0, BATCH, one_spread, 0)
+            lax.fori_loop(first, first + many, one_spread, 0)
+        spread_tail()
         total[...] = turned[...].T
         if step == 0:
             load.wait()
         collide(pops)
-        exchange(step)
-        stream(step)
+        copies = exchange(step)
+        stream(step, copies)
+        sample_tail()
         if step < STEPS - 1:
 
             def one_sample(g, _):
@@ -614,9 +659,11 @@
             pltpu.VMEM((WIDE, WIDE), BF16),
             pltpu.VMEM((1, WIDE), F32),
             pltpu.VMEM((16, WIDE), F32),
-            pltpu.VMEM((BATCH, 16, WIDE), F32),
+            pltpu.VMEM((GROUPS, 16, WIDE), F32),
             pltpu.VMEM((GROUPS, 8, LANES), F32),
+            pltpu.VMEM((8, 128), F32),
             pltpu.VMEM((GROUPS, plane, LANES), BF16),
+            pltpu.VMEM((plane, 128), BF16),
             pltpu.VMEM((3 * width_x, LANES), BF16),
             pltpu.VMEM((3 * width_x, plane), F32),
             pltpu.VMEM((plane, 3 * width_x), F32),

time: 82.4 us -> 77.2 us (0.937)
  Pallas kernels: 81.5 us -> 76.4 us
    pallas_call x1, Pallas kernels: 79.3 us -> 74.2 us  [local(): pl.pallas_call(functools.partial(kernel, nx, ny), out_shape=(jax.ShapeDty...]
where the time goes in v2:
time: 77.2 us; the launch traced here: 77 us
  Pallas kernels  76.4 us (99%)
    pallas_call x1, Pallas kernels, local(): pl.pallas_call(functools.partial(kernel, nx, ny), out_shape=(jax.ShapeDty...  74.2 us
    pallas_call x1, Pallas kernels, local(): pl.pallas_call(hand_out, out_shape=tuple((jax.ShapeDtypeStruct(r.shape, F...  2.23 us

profile of v2, /device:TPU:0, one launch (start us, length us, event | category | flops | bytes accessed | tf_op | source)
XLA Modules:
  0.0 77.0 jit_solution(2056072858982745172)
XLA Ops:
  0.6 74.2 %shard_map.85 = (f32[19,32,512]{2,1,0:T(8,128)}, f32[3,24,642]{2,1,0:T(8,128)}, f32[3,32,512]{2,1,0:T(8,128)}) custom-call(f32[19,32,512]{2,1,0:T(8,128)} %pops_ref.1, f32[3,24,642]{2,1,0:T(8,128)} %bitcast.5, f32[1,24]{1,0:T(1,128)} %bitcast.7, s32[1,24]{1,0:T(1,128)} %bitcast.8, f32[3,642]{1,0:T(4,128)} %shape_ref.1, s32[6,642]{1,0:T(8,128)} %bitcast.6), custom_call_target="tpu_custom_call" | custom-call | tf_op jit(solution)/shard_map/pallas_call | solution.py:637
  74.8 2.2 %shard_map.86 = (f32[19,32,512]{2,1,0:T(8,128)}, f32[3,24,642]{2,1,0:T(8,128)}, f32[3,32,512]{2,1,0:T(8,128)}) custom-call(f32[19,32,512]{2,1,0:T(8,128)} %get-tuple-element.9.a, f32[3,24,642]{2,1,0:T(8,128)} %get-tuple-element.10.b, f32[3,32,512]{2,1,0:T(8,128)} %get-tuple-element.11.c), custom_call_target="tpu_custom_call" | custom-call | tf_op jit(solution)/shard_map/pallas_call | solution.py:692

commit v3 on v2

--- a/solution.py
+++ b/solution.py
@@ -17,6 +17,8 @@
 MAIN = 640
 LANES = CAP * MAIN
 MESSAGE = 1024
+HALF = 16
+WINDOW = (HALF + 1) * CZ
 CHUNKS = [(start, 512) for start in range(0, LANES, 512)]
 
 VELOCITY = [
@@ -130,6 +132,7 @@
     flat_tail,
     table,
     table_tail,
+    window,
     lifted,
     total,
     turned,
@@ -313,13 +316,20 @@
             flat_tail[row + c : row + c + 1, :] = jnp.where(mine, tail, flat_tail[row + c : row + c + 1, :])
 
     def tabulate(read, put_table, put_lifted, at):
+        y = read(1, at)
+        low = y < HALF
         along_x = hat(read(0, at), 32, 0.0)
-        along_y = hat(read(1, at), 32, 0.0)
+        along_y = hat(y, 32, 0.0)
         along_z = hat_z(read(2, at))
         for j in range(32):
             put_table(j, at, (along_y[j : j + 1] * along_z).astype(BF16))
+        along_y = hat(jnp.where(low, y, y - HALF), 24, 0.0)
+        for j in range(HALF + 1):
+            window[CZ * j : CZ * j + CZ, at] = (along_y[j : j + 1] * along_z).astype(BF16)
         for c in range(3):
-            put_lifted(c, at, (read(3 + c, at) * along_x).astype(BF16))
+            force = read(3 + c, at)
+            put_lifted(c, at, (jnp.where(low, force, 0.0) * along_x).astype(BF16))
+            put_lifted(3 + c, at, (jnp.where(low, 0.0, force) * along_x).astype(BF16))
 
     def put_lifted(c, at, value):
         lifted[32 * c : 32 * c + 32, at] = value
@@ -333,8 +343,8 @@
 
         for t in range(0, LANES, 128):
             tabulate(lambda n, at: flat[g, n : n + 1, at], put_table, put_lifted, slice(t, t + 128))
-        turned[...] += lax.dot_general(
-            table[g], lifted[...], (((1,), (1,)), ((), ())), preferred_element_type=F32
+        turned[0:WINDOW, 0:192] += lax.dot_general(
+            window[...], lifted[...], (((1,), (1,)), ((), ())), preferred_element_type=F32
         )
 
     def spread_tail():
@@ -343,8 +353,8 @@
 
         at = slice(0, 128)
         tabulate(lambda n, at: flat_tail[n : n + 1, at], put_table, put_lifted, at)
-        turned[...] += lax.dot_general(
-            table_tail[...], lifted[:, at], (((1,), (1,)), ((), ())), preferred_element_type=F32
+        turned[0:WINDOW, 0:192] += lax.dot_general(
+            window[:, at], lifted[:, at], (((1,), (1,)), ((), ())), preferred_element_type=F32
         )
 
     def drifts(picked, row):
@@ -549,7 +559,10 @@
 
             lax.fori_loop(first, first + many, one_spread, 0)
         spread_tail()
-        total[...] = turned[...].T
+        grid = turned[...].T
+        total[:, 0:256] = grid[0:96, 0:256]
+        total[:, 256:384] = grid[96:192, 0:128] + grid[0:96, 256:384]
+        total[:, 384:512] = grid[96:192, 128:256]
         if step == 0:
             load.wait()
         collide(pops)
@@ -664,9 +677,10 @@
             pltpu.VMEM((8, 128), F32),
             pltpu.VMEM((GROUPS, plane, LANES), BF16),
             pltpu.VMEM((plane, 128), BF16),
-            pltpu.VMEM((3 * width_x, LANES), BF16),
+            pltpu.VMEM((WINDOW, LANES), BF16),
+            pltpu.VMEM((6 * width_x, LANES), BF16),
             pltpu.VMEM((3 * width_x, plane), F32),
-            pltpu.VMEM((plane, 3 * width_x), F32),
+            pltpu.VMEM((384, 256), F32),
             pltpu.VMEM(populations.shape, F32),
             pltpu.VMEM(populations.shape, F32),
             pltpu.VMEM((3 * width_x, plane), BF16),

time: 77.2 us -> 85.5 us (1.11)
  Pallas kernels: 76.4 us -> 84.5 us
    pallas_call x1, Pallas kernels: 74.2 us -> 82.3 us  [local(): pl.pallas_call(functools.partial(kernel, nx, ny), out_shape=(jax.ShapeDty...]
where the time goes in v3:
time: 85.5 us; the launch traced here: 85.3 us
  Pallas kernels  84.5 us (99%)
    pallas_call x1, Pallas kernels, local(): pl.pallas_call(functools.partial(kernel, nx, ny), out_shape=(jax.ShapeDty...  82.3 us
    pallas_call x1, Pallas kernels, local(): pl.pallas_call(hand_out, out_shape=tuple((jax.ShapeDtypeStruct(r.shape, F...  2.23 us

profile of v3, /device:TPU:0, one launch (start us, length us, event | category | flops | bytes accessed | tf_op | source)
XLA Modules:
  0.0 85.3 jit_solution(12083595170811065995)
XLA Ops:
  0.6 82.3 %shard_map.85 = (f32[19,32,512]{2,1,0:T(8,128)}, f32[3,24,642]{2,1,0:T(8,128)}, f32[3,32,512]{2,1,0:T(8,128)}) custom-call(f32[19,32,512]{2,1,0:T(8,128)} %pops_ref.1, f32[3,24,642]{2,1,0:T(8,128)} %bitcast.5, f32[1,24]{1,0:T(1,128)} %bitcast.7, s32[1,24]{1,0:T(1,128)} %bitcast.8, f32[3,642]{1,0:T(4,128)} %shape_ref.1, s32[6,642]{1,0:T(8,128)} %bitcast.6), custom_call_target="tpu_custom_call" | custom-call | tf_op jit(solution)/shard_map/pallas_call | solution.py:650
  82.9 2.2 %shard_map.86 = (f32[19,32,512]{2,1,0:T(8,128)}, f32[3,24,642]{2,1,0:T(8,128)}, f32[3,32,512]{2,1,0:T(8,128)}) custom-call(f32[19,32,512]{2,1,0:T(8,128)} %get-tuple-element.9.a, f32[3,24,642]{2,1,0:T(8,128)} %get-tuple-element.10.b, f32[3,32,512]{2,1,0:T(8,128)} %get-tuple-element.11.c), custom_call_target="tpu_custom_call" | custom-call | tf_op jit(solution)/shard_map/pallas_call | solution.py:706

commit v4 on v3

--- a/solution.py
+++ b/solution.py
@@ -132,13 +132,13 @@
     flat_tail,
     table,
     table_tail,
-    window,
     lifted,
     total,
     turned,
     pops,
     post,
     velocity,
+    windows,
     x_send,
     y_send,
     e_send,
@@ -319,13 +319,10 @@
         y = read(1, at)
         low = y < HALF
         along_x = hat(read(0, at), 32, 0.0)
-        along_y = hat(y, 32, 0.0)
+        along_y = hat(jnp.where(low, y, y - HALF), 24, 0.0)
         along_z = hat_z(read(2, at))
-        for j in range(32):
+        for j in range(HALF + 1):
             put_table(j, at, (along_y[j : j + 1] * along_z).astype(BF16))
-        along_y = hat(jnp.where(low, y, y - HALF), 24, 0.0)
-        for j in range(HALF + 1):
-            window[CZ * j : CZ * j + CZ, at] = (along_y[j : j + 1] * along_z).astype(BF16)
         for c in range(3):
             force = read(3 + c, at)
             put_lifted(c, at, (jnp.where(low, force, 0.0) * along_x).astype(BF16))
@@ -344,7 +341,7 @@
         for t in range(0, LANES, 128):
             tabulate(lambda n, at: flat[g, n : n + 1, at], put_table, put_lifted, slice(t, t + 128))
         turned[0:WINDOW, 0:192] += lax.dot_general(
-            window[...], lifted[...], (((1,), (1,)), ((), ())), preferred_element_type=F32
+            table[g], lifted[...], (((1,), (1,)), ((), ())), preferred_element_type=F32
         )
 
     def spread_tail():
@@ -354,27 +351,35 @@
         at = slice(0, 128)
         tabulate(lambda n, at: flat_tail[n : n + 1, at], put_table, put_lifted, at)
         turned[0:WINDOW, 0:192] += lax.dot_general(
-            window[:, at], lifted[:, at], (((1,), (1,)), ((), ())), preferred_element_type=F32
+            table_tail[...], lifted[:, at], (((1,), (1,)), ((), ())), preferred_element_type=F32
         )
 
-    def drifts(picked, row):
-        along_x = hat(row, 32, 0.0)
+    def drifts(picked, x, y):
+        along_x = hat(x, 32, 0.0)
+        low = y < HALF
         return [
-            jnp.sum(picked[32 * c : 32 * c + 32] * along_x, axis=0, keepdims=True) for c in range(3)
+            jnp.sum(
+                jnp.where(low, picked[32 * c : 32 * c + 32], picked[96 + 32 * c : 128 + 32 * c]) * along_x,
+                axis=0,
+                keepdims=True,
+            )
+            for c in range(3)
         ]
 
     def sample_tail():
-        picked = jnp.dot(velocity[...], table_tail[...], preferred_element_type=F32)
+        picked = jnp.dot(windows[:, 0:WINDOW], table_tail[...], preferred_element_type=F32)
         used = lax.broadcasted_iota(jnp.int32, (1, 128), 1) < 8 * GROUPS
-        for c, value in enumerate(drifts(picked, flat_tail[0:1, :])):
+        for c, value in enumerate(drifts(picked, flat_tail[0:1, :], flat_tail[1:2, :])):
             flat_tail[3 + c : 4 + c, :] = jnp.where(used, value, 0.0)
 
     def sample_group(g, add):
         lane = lax.broadcasted_iota(jnp.int32, (1, 128), 1)
         for start, width in CHUNKS:
             at = slice(start, start + width)
-            picked = jnp.dot(velocity[...], table[g, :, at], preferred_element_type=F32)
-            for c, value in enumerate(drifts(picked, flat[g, 0:1, at])):
+            picked = jnp.dot(
+                windows[:, 0:256], table[g, 0:256, at], preferred_element_type=F32
+            ) + jnp.dot(windows[:, 256:WINDOW], table[g, 256:WINDOW, at], preferred_element_type=F32)
+            for c, value in enumerate(drifts(picked, flat[g, 0:1, at], flat[g, 1:2, at])):
                 flat[g, 3 + c : 4 + c, at] = value
         for c in range(3):
             tail = pltpu.roll(flat_tail[3 + c : 4 + c, :], 128 - 8 * g, 1)
@@ -452,12 +457,15 @@
 
     def exchange(step):
         lane = lax.broadcasted_iota(jnp.int32, (32, 128), 1)
+        copies = halo_copies(step)
         for n, (q, row, column) in enumerate(EDGE_MOVERS):
             e_send[step, n] = post[q, row : row + 8, column : column + 128]
+            copies[4 + n].start()
         for side, (movers, row) in enumerate(((RIGHT_MOVERS, 31), (LEFT_MOVERS, 0))):
             x_send[step, side] = jnp.zeros((8, 512), F32)
             for n, q in enumerate(movers):
                 x_send[step, side, n : n + 1, :] = post[q, row : row + 1, :]
+            copies[side].start()
         for side, (movers, column, turn) in enumerate(
             ((UPWARD_MOVERS, 384, 16), (DOWNWARD_MOVERS, 0, 0))
         ):
@@ -469,9 +477,7 @@
                     value = pltpu.roll(value, shift, 1)
                 face = jnp.where((lane >= 16 * n) & (lane < 16 * n + 16), value, face)
             y_send[step, side] = face
-        copies = halo_copies(step)
-        for copy in copies:
-            copy.start()
+            copies[2 + side].start()
         return copies
 
     def shift_rows(value, dx, edge):
@@ -568,6 +574,9 @@
         collide(pops)
         copies = exchange(step)
         stream(step, copies)
+        windows[0:96, 0:384] = velocity[:, 0:384]
+        windows[96:192, 0:256] = velocity[:, 256:512]
+        windows[96:192, 256:384] = jnp.zeros((96, 128), BF16)
         sample_tail()
         if step < STEPS - 1:
 
@@ -675,15 +684,15 @@
             pltpu.VMEM((GROUPS, 16, WIDE), F32),
             pltpu.VMEM((GROUPS, 8, LANES), F32),
             pltpu.VMEM((8, 128), F32),
-            pltpu.VMEM((GROUPS, plane, LANES), BF16),
-            pltpu.VMEM((plane, 128), BF16),
-            pltpu.VMEM((WINDOW, LANES), BF16),
+            pltpu.VMEM((GROUPS, WINDOW, LANES), BF16),
+            pltpu.VMEM((WINDOW, 128), BF16),
             pltpu.VMEM((6 * width_x, LANES), BF16),
             pltpu.VMEM((3 * width_x, plane), F32),
             pltpu.VMEM((384, 256), F32),
             pltpu.VMEM(populations.shape, F32),
             pltpu.VMEM(populations.shape, F32),
             pltpu.VMEM((3 * width_x, plane), BF16),
+            pltpu.VMEM((6 * width_x, 384), BF16),
             pltpu.VMEM((STEPS, 2, 8, plane), F32),
             pltpu.VMEM((STEPS, 2, width_x, 128), F32),
             pltpu.VMEM((STEPS, 4, 8, 128), F32),

time: 85.5 us -> 75.6 us (0.88)
  Pallas kernels: 84.5 us -> 74.8 us
    pallas_call x1, Pallas kernels: 82.3 us -> 72.6 us  [local(): pl.pallas_call(functools.partial(kernel, nx, ny), out_shape=(jax.ShapeDty...]
where the time goes in v4:
time: 75.6 us; the launch traced here: 75.4 us
  Pallas kernels  74.8 us (99%)
    pallas_call x1, Pallas kernels, local(): pl.pallas_call(functools.partial(kernel, nx, ny), out_shape=(jax.ShapeDty...  72.6 us
    pallas_call x1, Pallas kernels, local(): pl.pallas_call(hand_out, out_shape=tuple((jax.ShapeDtypeStruct(r.shape, F...  2.23 us

profile of v4, /device:TPU:0, one launch (start us, length us, event | category | flops | bytes accessed | tf_op | source)
XLA Modules:
  0.0 75.4 jit_solution(6100908602820559909)
XLA Ops:
  0.6 72.6 %shard_map.85 = (f32[19,32,512]{2,1,0:T(8,128)}, f32[3,24,642]{2,1,0:T(8,128)}, f32[3,32,512]{2,1,0:T(8,128)}) custom-call(f32[19,32,512]{2,1,0:T(8,128)} %pops_ref.1, f32[3,24,642]{2,1,0:T(8,128)} %bitcast.5, f32[1,24]{1,0:T(1,128)} %bitcast.7, s32[1,24]{1,0:T(1,128)} %bitcast.8, f32[3,642]{1,0:T(4,128)} %shape_ref.1, s32[6,642]{1,0:T(8,128)} %bitcast.6), custom_call_target="tpu_custom_call" | custom-call | tf_op jit(solution)/shard_map/pallas_call | solution.py:659
  73.2 2.2 %shard_map.86 = (f32[19,32,512]{2,1,0:T(8,128)}, f32[3,24,642]{2,1,0:T(8,128)}, f32[3,32,512]{2,1,0:T(8,128)}) custom-call(f32[19,32,512]{2,1,0:T(8,128)} %get-tuple-element.9.a, f32[3,24,642]{2,1,0:T(8,128)} %get-tuple-element.10.b, f32[3,32,512]{2,1,0:T(8,128)} %get-tuple-element.11.c), custom_call_target="tpu_custom_call" | custom-call | tf_op jit(solution)/shard_map/pallas_call | solution.py:715
